TPU v7x, 32 devices: a whole 2x2x4 slice. The times are simulated.
32 devices in a mesh: gx: 8 (over y, x, core), gy: 4 (over z).
Axes of the slice: x: 2, y: 2, z: 4, core: 2. Of those that a mesh axis runs over, the one named last changes fastest.
Arguments:
- velocity: float32 [3, 64, 64, 128], P(None, 'gx', 'gy'), may hold values from -6 to 6
- marker_force: float32 [3, 4096, 128], P(None, ('gx', 'gy')), may hold values from -6 to 6
- marker_cell: int32 [4096, 128], P(('gx', 'gy')), may hold values from 0 to 16383
- block_brick: int32 [4096, 1], P(('gx', 'gy')), may hold values from 0 to 31; in each aligned block of 128 rows (0 to 127, 128 to 255, ...) at most 8 rows name the same one
Outputs:
- velocity_new: float32 [3, 64, 64, 128], P(None, 'gx', 'gy')
- marker_velocity: float32 [3, 4096, 128], P(None, ('gx', 'gy'))
Inputs may be any that keep to these rules, and one draw needn't show every extreme that they name: `block_brick`: among the 128 blocks of one device no brick is named by more than 8 blocks, and some device names some brick exactly 8 times.
All inputs are finite; a program needn't handle non-finite values.
Results may differ from a plain program's by a relative error of at most 0.0003.
Values sent between devices are 32-bit elements; how exact they have to be, the bound alone decides.
A program may use at most 128 MiB of HBM per device.

v0:
```python
import jax
import jax.numpy as jnp
from jax import lax
from jax.sharding import PartitionSpec as P

SWEEPS = 4
DEPTH = 2
STEPS = 2


time_step = 0.5
viscosity = 0.2
stiffness = 1.0


def with_halo(block, sides, width):
    for axis, dim in sides:
        count = lax.axis_size(axis)
        forward = [(i, i + 1) for i in range(count - 1)]
        backward = [(target, source) for source, target in forward]
        low = lax.ppermute(
            lax.slice_in_dim(block, block.shape[dim] - width, None, axis=dim), axis, forward
        )
        high = lax.ppermute(lax.slice_in_dim(block, 0, width, axis=dim), axis, backward)
        block = jnp.concatenate([low, block, high], axis=dim)
    return block


def neighbours(grid_field):
    padded = jnp.pad(grid_field, [(0, 0)] * (grid_field.ndim - 3) + [(1, 1)] * 3)
    total_sum = padded[..., 2:, 1:-1, 1:-1] + padded[..., :-2, 1:-1, 1:-1]
    total_sum = total_sum + padded[..., 1:-1, 2:, 1:-1] + padded[..., 1:-1, :-2, 1:-1]
    return total_sum + padded[..., 1:-1, 1:-1, 2:] + padded[..., 1:-1, 1:-1, :-2]


def central(grid_field, direction):
    position = grid_field.ndim - 3 + direction
    widths = [(0, 0)] * grid_field.ndim
    widths[position] = (1, 1)
    padded = jnp.pad(grid_field, widths)
    length = padded.shape[position]
    forward = lax.slice_in_dim(padded, 2, length, axis=position)
    behind = lax.slice_in_dim(padded, 0, length - 2, axis=position)
    return 0.5 * (forward - behind)


def inner_part(grid_field, margin):
    return grid_field[
        ..., margin : grid_field.shape[-3] - margin, margin : grid_field.shape[-2] - margin, :
    ]


def inside_mask(margin, size_x, size_y):
    row_index = (
        lax.axis_index("gx") * size_x + jnp.arange(size_x + 2 * margin, dtype=jnp.int32) - margin
    )
    col_index = (
        lax.axis_index("gy") * size_y + jnp.arange(size_y + 2 * margin, dtype=jnp.int32) - margin
    )
    keep_rows = (row_index >= 0) & (row_index < size_x * lax.axis_size("gx"))
    keep_cols = (col_index >= 0) & (col_index < size_y * lax.axis_size("gy"))
    return (keep_rows[:, None] & keep_cols[None, :]).astype(jnp.float32)[:, :, None]


def pressure_rim(pressure, margin):
    return with_halo(pressure, (("gx", 0), ("gy", 1)), margin)


def advance(current, spread, flow_width, pressure_width, rounds, inner_sweeps):
    size_x, size_y = (current.shape[1], current.shape[2])
    stacked = jnp.concatenate([current, spread], axis=0)
    widened = with_halo(stacked, (("gx", 1), ("gy", 2)), flow_width)
    moving = widened[:3]
    provisional = moving + time_step * (
        viscosity * (neighbours(moving) - 6.0 * moving) + widened[3:]
    )
    provisional = inner_part(provisional * inside_mask(flow_width, size_x, size_y), 1)
    source = central(provisional[0], 0) + central(provisional[1], 1) + central(provisional[2], 2)
    source = inner_part(source, 1) / time_step
    keep_mask = inside_mask(pressure_width, size_x, size_y)
    pressure = jnp.zeros(current.shape[1:], jnp.float32)
    for turn_number in range(rounds):
        extended = pressure_rim(pressure, pressure_width)
        for sweep_number in range(inner_sweeps):
            extended = keep_mask * (neighbours(extended) - source) / 6.0
        pressure = inner_part(extended, pressure_width)
    extended = inner_part(pressure_rim(pressure, pressure_width), pressure_width - 1)
    slope = jnp.stack([central(extended, 0), central(extended, 1), central(extended, 2)])
    slope = inner_part(slope, 1)
    return inner_part(provisional, flow_width - 1) - time_step * slope


def send_blocks(outgoing, devices, capacity):
    width_mark = outgoing.shape[-1]
    shaped = outgoing.reshape(4, devices, capacity, width_mark)
    arrived = lax.all_to_all(shaped, ("gx", "gy"), split_axis=1, concat_axis=1, tiled=True)
    return arrived.reshape(4, devices * capacity, width_mark)


def send_back(picked, devices, capacity):
    width_mark = picked.shape[-1]
    shaped = picked.reshape(3, devices, capacity, width_mark)
    arrived = lax.all_to_all(shaped, ("gx", "gy"), split_axis=1, concat_axis=1, tiled=True)
    return arrived.reshape(3, devices * capacity, width_mark)


def body(velocity, marker_force, marker_cell, block_brick):
    devices = lax.axis_size("gx") * lax.axis_size("gy")
    blocks, width_mark = marker_cell.shape
    capacity = 2 * blocks // devices
    slot_count = devices * capacity
    pressure_width = DEPTH
    rounds = SWEEPS // DEPTH
    inner_sweeps = DEPTH
    flow_width = DEPTH + 2
    dest_brick = block_brick[:, 0]
    chosen = (dest_brick[:, None] == jnp.arange(devices, dtype=jnp.int32)[None, :]).astype(
        jnp.int32
    )
    earlier = jnp.sum((jnp.cumsum(chosen, axis=0) - chosen) * chosen, axis=1)
    target = dest_brick * capacity + earlier
    packed = jnp.concatenate([marker_force, marker_cell.astype(jnp.float32)[None]], axis=0)
    outgoing = jnp.zeros((4, slot_count, width_mark), jnp.float32).at[3].set(-1.0)
    outgoing = outgoing.at[:, target].set(packed)
    arrived = send_blocks(outgoing, devices, capacity)
    cell_number = arrived[3].astype(jnp.int32)
    live_slot = (cell_number >= 0).astype(jnp.float32)
    cell_flat = jnp.maximum(cell_number, 0).reshape(-1)
    held_force = arrived[:3] * live_slot
    current = velocity
    picked = held_force
    cell_total = velocity.shape[1] * velocity.shape[2] * velocity.shape[3]
    for step_number in range(STEPS):
        spread = (
            jnp.zeros((3, cell_total), jnp.float32).at[:, cell_flat].add(held_force.reshape(3, -1))
        )
        spread = spread.reshape(velocity.shape)
        current = advance(current, spread, flow_width, pressure_width, rounds, inner_sweeps)
        picked = current.reshape(3, -1)[:, cell_flat].reshape(held_force.shape)
        if step_number + 1 < STEPS:
            held_force = (held_force - stiffness * picked) * live_slot
    returned = send_back(picked, devices, capacity)
    return (current, returned[:, target])


def solution(mesh):
    return jax.shard_map(
        body,
        mesh=mesh,
        in_specs=(
            P(None, "gx", "gy", None),
            P(None, ("gx", "gy"), None),
            P(("gx", "gy"), None),
            P(("gx", "gy"), None),
        ),
        out_specs=(P(None, "gx", "gy", None), P(None, ("gx", "gy"), None)),
        check_vma=False,
    )
```

profile of v0, /device:TPU:1, one launch (start us, length us, event | category | flops | bytes accessed | tf_op | source)
XLA Modules:
  0.0 1720.7 jit_solution(440170180287554633)
XLA Ops:
  6.9 12.6 scatter_fusion
  19.5 7.1 all-to-all-start
  32.3 9.6 all-to-all-done
  41.9 8.2 copy.21
  50.3 12.7 bitcast_multiply_fusion
  63.2 205.2 %scatter_custom_fusion.1 = f32[3,16384]{0,1:T(8,128)} fusion(s32[32768]{0:T(1024)S(1)} %bitcast.73, f32[3,32768]{0,1:T(8,128)} %bitcast_multiply_fusion, f32[]{:T(128)} %constant.88.clone.1), kind=kCustom, calls=%fused_computation.10 | custom fusion | flops 98304 | bytes 589828 | tf_op jit(solution)/shard_map/scatter-add | solution.py:135
  268.3 5.3 copy.22
  280.6 8.3 collective-permute-start.6
  309.4 4.7 collective-permute-start.10
  317.6 5.1 collective-permute-start.12
  324.8 4.8 collective-permute-start.14
  330.5 4.7 copy.23
  335.2 1052.7 %scatter_custom_fusion.2 = f32[3,16384]{0,1:T(8,128)} fusion(s32[32768]{0:T(1024)S(1)} %bitcast.75, f32[3,32768]{0,1:T(8,128)} %bitcast_multiply_fusion, f32[32768]{0:T(1024)S(1)} %bitcast.70, f32[]{:T(128)} %constant.88.clone.1, f32[3,16384]{0,1:T(8,128)} %bitcast.64, s32[32768]{0:T(1024)S(1)} %broadcast_clamp_fusion), kind=kCustom, calls=%fused_computation.6 | custom fusion | flops 294912 | bytes 1048580 | tf_op jit(solution)/shard_map/scatter-add | solution.py:135
  1387.9 5.2 copy.24
  1402.7 97.9 %collective-permute-start.18 = (f32[6,16,4,128]{3,2,1,0:T(4,128)S(1)}, f32[6,16,4,128]{3,2,1,0:T(4,128)S(1)}, u32[]{:S(2)}, u32[]{:S(2)}) collective-permute-start(f32[6,16,4,128]{3,2,1,0:T(4,128)S(1)} %get-tuple-element.23), channel_id=1, source_target_pairs={{0,1},{1,2},{2,3},{4,5},{5,6},{6,7},{8,9},{9,10},{10,11},{12,13},{... | collective-permute-start | bytes 589832 | tf_op jit(solution)/shard_map/ppermute | solution.py:21
  1506.9 14.0 collective-permute-start.20
  1523.1 18.2 %collective-permute-start.22 = (f32[12,2,128]{2,1,0:T(2,128)S(1)}, f32[12,2,128]{2,1,0:T(2,128)S(1)}, u32[]{:S(2)}, u32[]{:S(2)}) collective-permute-start(f32[12,2,128]{2,1,0:T(2,128)S(1)} %get-tuple-element.65), channel_id=1, source_target_pairs={{0,1},{1,2},{2,3},{4,5},{5,6},{6,7},{8,9},{9,10},{10,11},{12,13},{... | collective-permute-start | bytes 36872 | tf_op jit(solution)/shard_map/ppermute | solution.py:21
  1544.8 6.1 collective-permute-start.24
  1553.0 4.5 collective-permute-start.26
  1558.6 4.7 copy.25
  1563.3 112.4 %gather_fusion = f32[32768,3]{1,0:T(8,128)} fusion(f32[3,16384]{0,1:T(8,128)} %bitcast.66, s32[32768]{0:T(1024)S(1)} %broadcast_clamp_fusion), kind=kCustom, calls=%fused_computation.1 | custom fusion | bytes 917504 | tf_op jit(solution)/shard_map/gather | solution.py:139
  1675.7 10.4 copy.26
  1686.0 20.3 %all-to-all-start.1 = ((f32[3,32,8,128]{3,2,0,1:T(8,128)}), f32[3,32,8,128]{3,2,0,1:T(8,128)S(1)}, u32[]{:S(2)}, u32[]{:S(2)}) async-start(f32[3,32,8,128]{3,2,0,1:T(8,128)} %copy.26), calls=%async_computation.1 | async-start | bytes 786432 | tf_op jit(solution)/shard_map/all_to_all | solution.py:103
  1706.4 12.7 all-to-all-done.1
  (121 shorter events, 72.0 us)
Async XLA Ops:
  19.5 22.4 %all-to-all-start = ((f32[4,32,8,128]{3,0,2,1:T(4,128)}), f32[4,32,8,128]{3,0,2,1:T(4,128)S(1)}, u32[]{:S(2)}, u32[]{:S(2)}) async-start(f32[4,32,8,128]{3,0,2,1:T(4,128)} %bitcast.5), calls=%async_computation | async-start | bytes 1048576 | tf_op jit(solution)/shard_map/all_to_all | solution.py:96
  26.6 252.6 %collective-permute-start.5 = (f32[2,16,128]{2,1,0:T(8,128)S(1)}, f32[2,16,128]{2,1,0:T(8,128)S(1)}, u32[]{:S(2)}, u32[]{:S(2)}) collective-permute-start(f32[2,16,128]{2,1,0:T(8,128)S(1)} %broadcast.312), channel_id=1, source_target_pairs={{4,0},{8,4},{12,8},{16,12},{20,16},{24,20},{28,24},{5,1},{9,5},{13... | collective-permute-start | bytes 49160 | tf_op jit(solution)/shard_map/ppermute | solution.py:24
  28.8 250.5 %collective-permute-start.4 = (f32[2,16,128]{2,1,0:T(8,128)S(1)}, f32[2,16,128]{2,1,0:T(8,128)S(1)}, u32[]{:S(2)}, u32[]{:S(2)}) collective-permute-start(f32[2,16,128]{2,1,0:T(8,128)S(1)} %broadcast.312), channel_id=1, source_target_pairs={{0,4},{4,8},{8,12},{12,16},{16,20},{20,24},{24,28},{1,5},{5,9},{9,... | collective-permute-start | bytes 49160 | tf_op jit(solution)/shard_map/ppermute | solution.py:21
  273.6 15.3 collective-permute-start.1
  275.6 13.4 collective-permute-start
  279.3 15.1 collective-permute-start.7
  280.6 13.8 collective-permute-start.6
  289.0 7.5 collective-permute-start.3
  290.3 7.1 collective-permute-start.2
  298.9 8.3 collective-permute-start.9
  308.1 6.0 collective-permute-start.11
  315.7 7.0 collective-permute-start.13
  323.5 6.2 collective-permute-start.15
  1393.2 7.0 collective-permute-start.17
  1395.1 6.2 collective-permute-start.16
  1401.4 100.5 %collective-permute-start.19 = (f32[6,16,4,128]{3,2,1,0:T(4,128)S(1)}, f32[6,16,4,128]{3,2,1,0:T(4,128)S(1)}, u32[]{:S(2)}, u32[]{:S(2)}) collective-permute-start(f32[6,16,4,128]{3,2,1,0:T(4,128)S(1)} %get-tuple-element.24), channel_id=1, source_target_pairs={{1,0},{2,1},{3,2},{5,4},{6,5},{7,6},{9,8},{10,9},{11,10},{13,12},{... | collective-permute-start | bytes 589832 | tf_op jit(solution)/shard_map/ppermute | solution.py:24
  1402.7 101.0 %collective-permute-start.18 = (f32[6,16,4,128]{3,2,1,0:T(4,128)S(1)}, f32[6,16,4,128]{3,2,1,0:T(4,128)S(1)}, u32[]{:S(2)}, u32[]{:S(2)}) collective-permute-start(f32[6,16,4,128]{3,2,1,0:T(4,128)S(1)} %get-tuple-element.23), channel_id=1, source_target_pairs={{0,1},{1,2},{2,3},{4,5},{5,6},{6,7},{8,9},{9,10},{10,11},{12,13},{... | collective-permute-start | bytes 589832 | tf_op jit(solution)/shard_map/ppermute | solution.py:21
  1505.0 15.9 collective-permute-start.21
  1506.9 14.8 collective-permute-start.20
  1521.8 19.5 %collective-permute-start.23 = (f32[12,2,128]{2,1,0:T(2,128)S(1)}, f32[12,2,128]{2,1,0:T(2,128)S(1)}, u32[]{:S(2)}, u32[]{:S(2)}) collective-permute-start(f32[12,2,128]{2,1,0:T(2,128)S(1)} %get-tuple-element.66), channel_id=1, source_target_pairs={{1,0},{2,1},{3,2},{5,4},{6,5},{7,6},{9,8},{10,9},{11,10},{13,12},{... | collective-permute-start | bytes 36872 | tf_op jit(solution)/shard_map/ppermute | solution.py:24
  1523.1 19.0 %collective-permute-start.22 = (f32[12,2,128]{2,1,0:T(2,128)S(1)}, f32[12,2,128]{2,1,0:T(2,128)S(1)}, u32[]{:S(2)}, u32[]{:S(2)}) collective-permute-start(f32[12,2,128]{2,1,0:T(2,128)S(1)} %get-tuple-element.65), channel_id=1, source_target_pairs={{0,1},{1,2},{2,3},{4,5},{5,6},{6,7},{8,9},{9,10},{10,11},{12,13},{... | collective-permute-start | bytes 36872 | tf_op jit(solution)/shard_map/ppermute | solution.py:21
  1542.9 8.0 collective-permute-start.25
  1544.8 6.9 collective-permute-start.24
  1686.0 33.1 %all-to-all-start.1 = ((f32[3,32,8,128]{3,2,0,1:T(8,128)}), f32[3,32,8,128]{3,2,0,1:T(8,128)S(1)}, u32[]{:S(2)}, u32[]{:S(2)}) async-start(f32[3,32,8,128]{3,2,0,1:T(8,128)} %copy.26), calls=%async_computation.1 | async-start | bytes 786432 | tf_op jit(solution)/shard_map/all_to_all | solution.py:103
  (8 other events, 166.1 us)
where the time goes:
time: 1720 us
  other arithmetic  1280 us (74%)
  starting transfers between devices  235 us (14%)
  local copies, waits for them, and re-layouts  168 us (10%)
  waiting for transfers between devices  37 us (2%)
    scatter-add x2, other arithmetic, body(): jnp.zeros((3, cell_total), jnp.float32).at[:, cell_flat]  1260 us
    ppermute x14, starting transfers between devices, with_halo(): lax.ppermute(lax.slice_in_dim(block, block.shape[dim] - width, None, axis...  183 us
    gather x1, local copies, waits for them, and re-layouts, body(): picked = current.reshape(3, -1)[:, cell_flat].reshape(held_force.shape)  112 us
  transfers between devices with their start and end apart: 30, of which 16 were waited for; matrix products, arithmetic and copies ran while one was open for 14% of the time, Pallas kernels for 0%

commit v1 on v0

v1 whole, which is shorter than its diff:
```python
import functools

import jax
import jax.numpy as jnp
from jax import lax
from jax.experimental import pallas as pl
from jax.experimental.pallas import tpu as pltpu
from jax.sharding import PartitionSpec as P

SWEEPS = 4
STEPS = 2
MESH = pl.DeviceIdType.MESH

time_step = 0.5
viscosity = 0.2
stiffness = 1.0

HALO_X = SWEEPS + 2
HALO_Y = 8

BF = jnp.bfloat16
VMEM = pl.BlockSpec(memory_space=pltpu.VMEM)
SMEM = pl.BlockSpec(memory_space=pltpu.SMEM)
DIRECTIONS = [(i, j) for i in (-1, 0, 1) for j in (-1, 0, 1) if (i, j) != (0, 0)]


def pack_kernel(devices, cap, brick_ref, force_ref, cell_ref, out_ref, dest_ref, rank_ref, seen):
    blocks, width = cell_ref.shape
    out_ref[:, : 3 * cap, :] = jnp.zeros((devices, 3 * cap, width), jnp.float32)
    out_ref[:, 3 * cap :, :] = jnp.full((devices, cap, width), -1.0, jnp.float32)

    def clear(i, carry):
        seen[i] = 0
        return carry

    lax.fori_loop(0, devices, clear, 0)

    def place(b, carry):
        dest = brick_ref[b]
        rank = seen[dest]
        seen[dest] = rank + 1
        dest_ref[b] = dest
        rank_ref[b] = rank
        for c in range(3):
            out_ref[dest, pl.ds(c * cap + rank, 1), :] = force_ref[c, pl.ds(b, 1), :]
        out_ref[dest, pl.ds(3 * cap + rank, 1), :] = cell_ref[pl.ds(b, 1), :].astype(jnp.float32)
        return carry

    lax.fori_loop(0, blocks, place, 0, unroll=4)


def peer_of(me, k, devices, n_gy):
    peer = lax.rem(me + k, devices)
    return (peer // n_gy, lax.rem(peer, n_gy))


def exchange_kernel(devices, n_gy, src_ref, dst_ref, send_sem, recv_sem, own_sem):
    me = lax.axis_index("gx") * n_gy + lax.axis_index("gy")
    barrier = pltpu.get_barrier_semaphore()

    def greet(k, carry):
        pl.semaphore_signal(
            barrier, inc=1, device_id=peer_of(me, k, devices, n_gy), device_id_type=MESH
        )
        return carry

    lax.fori_loop(1, devices, greet, 0)
    own = pltpu.make_async_copy(src_ref.at[me], dst_ref.at[me], own_sem)
    own.start()
    pl.semaphore_wait(barrier, devices - 1)

    def copy_to(k):
        return pltpu.make_async_remote_copy(
            src_ref=src_ref.at[lax.rem(me + k, devices)],
            dst_ref=dst_ref.at[me],
            send_sem=send_sem.at[k],
            recv_sem=recv_sem.at[k],
            device_id=peer_of(me, k, devices, n_gy),
            device_id_type=MESH,
        )

    def copy_from(k):
        sender = lax.rem(me + devices - k, devices)
        return pltpu.make_async_remote_copy(
            src_ref=src_ref.at[sender],
            dst_ref=dst_ref.at[sender],
            send_sem=send_sem.at[k],
            recv_sem=recv_sem.at[k],
            device_id=peer_of(me, k, devices, n_gy),
            device_id_type=MESH,
        )

    def begin(k, carry):
        copy_to(k).start()
        return carry

    def finish(k, carry):
        copy_from(k).wait_recv()
        return carry

    def drain(k, carry):
        copy_to(k).wait_send()
        return carry

    lax.fori_loop(1, devices, begin, 0)
    lax.fori_loop(1, devices, finish, 0)
    lax.fori_loop(1, devices, drain, 0)
    own.wait()


def exchange(sent, devices, n_gy, number):
    return pl.pallas_call(
        functools.partial(exchange_kernel, devices, n_gy),
        out_shape=jax.ShapeDtypeStruct(sent.shape, sent.dtype),
        in_specs=[VMEM],
        out_specs=VMEM,
        scratch_shapes=[
            pltpu.SemaphoreType.DMA((devices,)),
            pltpu.SemaphoreType.DMA((devices,)),
            pltpu.SemaphoreType.DMA,
        ],
        compiler_params=pltpu.CompilerParams(
            collective_id=number, has_side_effects=True, vmem_limit_bytes=32 << 20
        ),
    )(sent)


def cell_parts(cells, half, depth):
    row = cells // depth
    short = jnp.where(cells < 0, -1, lax.rem(row, half))
    long = (row // half) * depth + lax.rem(cells, depth)
    return short.astype(jnp.float32), long.astype(jnp.float32)


def tall(row):
    return jnp.broadcast_to(row, (16, row.shape[1])).astype(BF)


def one_hot_mask(row, size):
    shape = (size // 16, 16, row.shape[1])
    index = lax.broadcasted_iota(jnp.int32, shape, 0) * 16 + lax.broadcasted_iota(jnp.int32, shape, 1)
    return index.astype(jnp.float32).astype(BF) == tall(row)[None]


def spread_kernel(cap, group, half, depth, in_ref, out_ref, acc):
    count = in_ref.shape[0]
    width = in_ref.shape[2]
    acc[...] = jnp.zeros_like(acc)

    def one(i, carry):
        lefts, rights = [], []
        for g in range(group):
            block = in_ref[i * group + g]
            short, long = cell_parts(block[3 * cap :].astype(jnp.int32), half, depth)
            high = block[: 3 * cap].astype(BF).astype(jnp.float32)
            low = block[: 3 * cap] - high
            for e in range(cap):
                mask = one_hot_mask(short[e : e + 1], half)
                zero = jnp.zeros((16, width), BF)
                one_ = jnp.ones((16, width), BF)
                pieces = []
                for part in (high, low):
                    for c in range(3):
                        value = tall(part[c * cap + e : c * cap + e + 1])
                        pieces.append(jnp.where(mask, value[None], zero[None]).reshape(half, width))
                pieces.append(jnp.where(mask, one_[None], zero[None]).reshape(half, width))
                lefts.append(jnp.concatenate(pieces, axis=0))
                spot = one_hot_mask(long[e : e + 1], 2 * depth)
                rights.append(jnp.where(spot, one_[None], zero[None]).reshape(2 * depth, width))
        left = jnp.concatenate(lefts, axis=1)
        right = jnp.concatenate(rights, axis=1)
        acc[...] += lax.dot_general(
            left, right, (((1,), (1,)), ((), ())), preferred_element_type=jnp.float32
        )
        return carry

    lax.fori_loop(0, count // group, one, 0)
    for c in range(4):
        if c < 3:
            total = acc[c * half : (c + 1) * half] + acc[(3 + c) * half : (4 + c) * half]
        else:
            total = acc[6 * half : 7 * half]
        out_ref[c, :half, :] = total[:, :depth]
        out_ref[c, half:, :] = total[:, depth:]


def pick_kernel(cap, group, half, depth, in_ref, flow_ref, out_ref):
    count = in_ref.shape[0]
    width = in_ref.shape[2]
    table = jnp.concatenate(
        [jnp.concatenate([flow_ref[c, :half], flow_ref[c, half:]], axis=1) for c in range(3)], axis=0
    )
    high = table.astype(BF)
    low = (table - high.astype(jnp.float32)).astype(BF)
    table = jnp.concatenate([high, low], axis=0)
    index = lax.broadcasted_iota(jnp.int32, (half, width), 0).astype(jnp.float32)

    def one(i, carry):
        rights, shorts = [], []
        for g in range(group):
            cells = in_ref[i * group + g, 3 * cap :, :].astype(jnp.int32)
            short, long = cell_parts(cells, half, depth)
            for e in range(cap):
                spot = one_hot_mask(long[e : e + 1], 2 * depth)
                one_ = jnp.ones((16, width), BF)[None]
                zero = jnp.zeros((16, width), BF)[None]
                rights.append(jnp.where(spot, one_, zero).reshape(2 * depth, width))
                shorts.append(short[e : e + 1])
        both = jnp.dot(table, jnp.concatenate(rights, axis=1), preferred_element_type=jnp.float32)
        for g in range(group):
            rows = []
            for c in range(3):
                for e in range(cap):
                    n = g * cap + e
                    cut = both[:, n * width : (n + 1) * width]
                    value = cut[c * half : (c + 1) * half] + cut[(3 + c) * half : (4 + c) * half]
                    mask = index == shorts[n]
                    rows.append(jnp.sum(jnp.where(mask, value, 0.0), axis=0, keepdims=True))
            out_ref[i * group + g] = jnp.concatenate(rows, axis=0)
        return carry

    lax.fori_loop(0, count // group, one, 0)


def unpack_kernel(cap, dest_ref, rank_ref, in_ref, out_ref):
    blocks = out_ref.shape[1]

    def take(b, carry):
        dest = dest_ref[b]
        rank = rank_ref[b]
        for c in range(3):
            out_ref[c, pl.ds(b, 1), :] = in_ref[dest, pl.ds(c * cap + rank, 1), :]
        return carry

    lax.fori_loop(0, blocks, take, 0, unroll=4)


def flow_kernel(n_gx, n_gy, flow_ref, spread_ref, out_ref, wide, moved, later, send_sem, recv_sem):
    size_x, size_y, depth = flow_ref.shape[1:]
    gx, gy = lax.axis_index("gx"), lax.axis_index("gy")

    def exists(dx, dy):
        x, y = gx + dx, gy + dy
        return (x >= 0) & (x < n_gx) & (y >= 0) & (y < n_gy)

    def cut(d, size, halo):
        if d == 0:
            return (0, size), (halo, size)
        if d > 0:
            return (size - halo, halo), (0, halo)
        return (0, halo), (halo + size, halo)

    def copy(turn, number, src, first, fields):
        dx, dy = DIRECTIONS[number]
        (sx, nx), (tx, _) = cut(dx, size_x, HALO_X)
        (sy, ny), (ty, _) = cut(dy, size_y, HALO_Y)
        target = later if turn else wide
        return pltpu.make_async_remote_copy(
            src_ref=src.at[:, pl.ds(sx, nx), pl.ds(sy, ny), :],
            dst_ref=target.at[pl.ds(first, fields), pl.ds(tx, nx), pl.ds(ty, ny), :],
            send_sem=send_sem.at[turn, number],
            recv_sem=recv_sem.at[turn, number],
            device_id=(gx + dx, gy + dy),
            device_id_type=MESH,
        )

    barrier = pltpu.get_barrier_semaphore()
    for dx, dy in DIRECTIONS:

        @pl.when(exists(dx, dy))
        def _():
            pl.semaphore_signal(barrier, inc=1, device_id=(gx + dx, gy + dy), device_id_type=MESH)

    inner = (slice(HALO_X, HALO_X + size_x), slice(HALO_Y, HALO_Y + size_y))
    moved[:3] = flow_ref[...]
    moved[3:] = spread_ref[...].reshape(4, size_x, size_y, depth)
    span_x = 1 + exists(-1, 0).astype(jnp.int32) + exists(1, 0).astype(jnp.int32)
    span_y = 1 + exists(0, -1).astype(jnp.int32) + exists(0, 1).astype(jnp.int32)
    pl.semaphore_wait(barrier, span_x * span_y - 1)

    def run_exchange(turn, src, target, fields):
        for number, (dx, dy) in enumerate(DIRECTIONS):

            @pl.when(exists(dx, dy))
            def _():
                copy(turn, number, src, 0, fields).start()

            @pl.when(jnp.logical_not(exists(-dx, -dy)))
            def _():
                _, (tx, nx) = cut(dx, size_x, HALO_X)
                _, (ty, ny) = cut(dy, size_y, HALO_Y)
                target[:, tx : tx + nx, ty : ty + ny, :] = jnp.zeros(
                    (fields, nx, ny, depth), jnp.float32
                )

        target[:, inner[0], inner[1], :] = src[...]
        for number, (dx, dy) in enumerate(DIRECTIONS):

            @pl.when(exists(-dx, -dy))
            def _():
                copy(turn, number, src, 0, fields).wait_recv()

        for number, (dx, dy) in enumerate(DIRECTIONS):

            @pl.when(exists(dx, dy))
            def _():
                copy(turn, number, src, 0, fields).wait_send()

    wide_x, wide_y = size_x + 2 * HALO_X, size_y + 2 * HALO_Y
    place_x = lax.broadcasted_iota(jnp.int32, (wide_x, wide_y, depth), 0) + (gx * size_x - HALO_X)
    place_y = lax.broadcasted_iota(jnp.int32, (wide_x, wide_y, depth), 1) + (gy * size_y - HALO_Y)
    keep = (
        (place_x >= 0) & (place_x < n_gx * size_x) & (place_y >= 0) & (place_y < n_gy * size_y)
    ).astype(jnp.float32)
    level = lax.broadcasted_iota(jnp.int32, (1, wide_y, depth), 2)
    not_first = (level > 0).astype(jnp.float32)
    not_last = (level < depth - 1).astype(jnp.float32)

    def up_y(v):
        return pltpu.roll(v, wide_y - 1, 1)

    def down_y(v):
        return pltpu.roll(v, 1, 1)

    def up_z(v):
        return pltpu.roll(v, depth - 1, 2) * not_last

    def down_z(v):
        return pltpu.roll(v, 1, 2) * not_first

    def around(v):
        mid = v[1:-1]
        return (v[2:] + v[:-2]) + (up_y(mid) + down_y(mid)) + (up_z(mid) + down_z(mid))

    def advance(flow, force):
        provisional = []
        for c in range(3):
            mid = flow[c][1:-1]
            stepped = mid + time_step * (viscosity * (around(flow[c]) - 6.0 * mid) + force[c][1:-1])
            provisional.append(stepped * keep[1:-1])
        p0, p1, p2 = provisional
        source = (
            0.5 * (p0[2:] - p0[:-2])
            + 0.5 * (up_y(p1[1:-1]) - down_y(p1[1:-1]))
            + 0.5 * (up_z(p2[1:-1]) - down_z(p2[1:-1]))
        ) / time_step
        pressure = -source * keep[2:-2] / 6.0
        for sweep in range(1, SWEEPS):
            edge = sweep + 2
            pressure = (around(pressure) - source[sweep:-sweep]) * keep[edge:-edge] / 6.0
        mid = pressure[1:-1]
        slopes = (
            0.5 * (pressure[2:] - pressure[:-2]),
            0.5 * (up_y(mid) - down_y(mid)),
            0.5 * (up_z(mid) - down_z(mid)),
        )
        far = HALO_X - 1
        return [(provisional[c][far:-far] - time_step * slopes[c])[:, inner[1], :] for c in range(3)]

    run_exchange(0, moved, wide, 7)
    result = advance([wide[c] for c in range(3)], [wide[3 + c] for c in range(3)])
    for c in range(3):
        out_ref[c] = result[c]
    for turn in range(1, STEPS):
        run_exchange(turn, out_ref, later, 3)
        flow = [later[c] for c in range(3)]
        force = [wide[3 + c] - stiffness * wide[6] * flow[c] for c in range(3)]
        result = advance(flow, force)
        for c in range(3):
            out_ref[c] = result[c]


def body(n_gx, n_gy, velocity, marker_force, marker_cell, block_brick):
    devices = n_gx * n_gy
    blocks, width = marker_cell.shape
    size_x, size_y, depth = velocity.shape[1:]
    cap = 2 * blocks // devices
    rows = size_x * size_y
    half = rows // 2
    group = max(1, 8 // cap)
    sent, dest, rank = pl.pallas_call(
        functools.partial(pack_kernel, devices, cap),
        out_shape=(
            jax.ShapeDtypeStruct((devices, 4 * cap, width), jnp.float32),
            jax.ShapeDtypeStruct((blocks,), jnp.int32),
            jax.ShapeDtypeStruct((blocks,), jnp.int32),
        ),
        in_specs=[SMEM, VMEM, VMEM],
        out_specs=(VMEM, SMEM, SMEM),
        scratch_shapes=[pltpu.SMEM((devices,), jnp.int32)],
    )(block_brick.reshape(blocks), marker_force, marker_cell)
    held = exchange(sent, devices, n_gy, 0)
    spread = pl.pallas_call(
        functools.partial(spread_kernel, cap, group, half, depth),
        out_shape=jax.ShapeDtypeStruct((4, rows, depth), jnp.float32),
        in_specs=[VMEM],
        out_specs=VMEM,
        scratch_shapes=[pltpu.VMEM((7 * half, 2 * depth), jnp.float32)],
        compiler_params=pltpu.CompilerParams(vmem_limit_bytes=40 << 20),
    )(held)
    wide = (size_x + 2 * HALO_X, size_y + 2 * HALO_Y, depth)
    current = pl.pallas_call(
        functools.partial(flow_kernel, n_gx, n_gy),
        out_shape=jax.ShapeDtypeStruct(velocity.shape, jnp.float32),
        in_specs=[VMEM, VMEM],
        out_specs=VMEM,
        scratch_shapes=[
            pltpu.VMEM((7,) + wide, jnp.float32),
            pltpu.VMEM((7, size_x, size_y, depth), jnp.float32),
            pltpu.VMEM((3,) + wide, jnp.float32),
            pltpu.SemaphoreType.DMA((STEPS, 8)),
            pltpu.SemaphoreType.DMA((STEPS, 8)),
        ],
        compiler_params=pltpu.CompilerParams(
            collective_id=1, has_side_effects=True, vmem_limit_bytes=40 << 20
        ),
    )(velocity, spread)
    picked = pl.pallas_call(
        functools.partial(pick_kernel, cap, group, half, depth),
        out_shape=jax.ShapeDtypeStruct((devices, 3 * cap, width), jnp.float32),
        in_specs=[VMEM, VMEM],
        out_specs=VMEM,
        compiler_params=pltpu.CompilerParams(vmem_limit_bytes=40 << 20),
    )(held, current.reshape(3, rows, depth))
    returned = exchange(picked, devices, n_gy, 2)
    marker_velocity = pl.pallas_call(
        functools.partial(unpack_kernel, cap),
        out_shape=jax.ShapeDtypeStruct((3, blocks, width), jnp.float32),
        in_specs=[SMEM, SMEM, VMEM],
        out_specs=VMEM,
    )(dest, rank, returned)
    return current, marker_velocity


def solution(mesh):
    n_gx, n_gy = mesh.shape["gx"], mesh.shape["gy"]
    return jax.shard_map(
        functools.partial(body, n_gx, n_gy),
        mesh=mesh,
        in_specs=(
            P(None, "gx", "gy", None),
            P(None, ("gx", "gy"), None),
            P(("gx", "gy"), None),
            P(("gx", "gy"), None),
        ),
        out_specs=(P(None, "gx", "gy", None), P(None, ("gx", "gy"), None)),
        check_vma=False,
    )
```

time: 1720 us -> 98.8 us (0.06)
  other arithmetic: 1280 us -> 0 us
  starting transfers between devices: 235 us -> 0 us
  local copies, waits for them, and re-layouts: 168 us -> 2.46 us
  Pallas kernels: 0 us -> 95.3 us
  waiting for transfers between devices: 37 us -> 0 us
    scatter-add x2 -> x0, other arithmetic: 1260 us -> none  [body(): jnp.zeros((3, cell_total), jnp.float32).at[:, cell_flat]]
    ppermute x28 -> x0, starting transfers between devices: 207 us -> none  [the longest x14 183 us: with_halo(): lax.ppermute(lax.slice_in_dim(block, block.shape[dim] - width, None, axis...]
    gather x2 -> x0, local copies, waits for them, and re-layouts: 113 us -> none  [the longest x1 112 us: body(): picked = current.reshape(3, -1)[:, cell_flat].reshape(held_force.shape)]
    pallas_call x0 -> x7, Pallas kernels: none -> 95.3 us  [the longest x2 37.8 us: exchange(): pl.pallas_call(functools.partial(exchange_kernel, devices, n_gy), out_sha...]
    all_to_all x2 -> x0, starting transfers between devices: 27.4 us -> none  [the longest x1 20.3 us: send_back(): lax.all_to_all(shaped, ('gx', 'gy'), split_axis=1, concat_axis=1, tiled=T...]
    all_to_all x2 -> x0, waiting for transfers between devices: 22.3 us -> none  [the longest x1 12.7 us: send_back(): lax.all_to_all(shaped, ('gx', 'gy'), split_axis=1, concat_axis=1, tiled=T...]
  transfers between devices with their start and end apart: 30 -> 0, of which waited for: 16 -> 0; matrix products, arithmetic and copies ran while one was open for 14% -> 0% of each run, Pallas kernels for 0% -> 0%
where the time goes in v1:
time: 98.8 us; the launch traced here: 98.4 us
  Pallas kernels  95.3 us (96%)
  local copies, waits for them, and re-layouts  2.46 us (2%)
    pallas_call x2, Pallas kernels, exchange(): pl.pallas_call(functools.partial(exchange_kernel, devices, n_gy), out_sha...  37.8 us
    pallas_call x1, Pallas kernels, body(): pl.pallas_call(functools.partial(flow_kernel, n_gx, n_gy), out_shape=jax....  25 us
    pallas_call x1, Pallas kernels, body(): pl.pallas_call(functools.partial(spread_kernel, cap, group, half, depth),...  14.7 us
    pallas_call x1, Pallas kernels, body(): pl.pallas_call(functools.partial(pick_kernel, cap, group, half, depth), o...  13 us
    pallas_call x1, Pallas kernels, body(): pl.pallas_call(functools.partial(pack_kernel, devices, cap), out_shape=(j...  2.69 us
    unnamed x7, local copies, waits for them, and re-layouts  2.46 us
    pallas_call x1, Pallas kernels, body(): pl.pallas_call(functools.partial(unpack_kernel, cap), out_shape=jax.Shape...  2.07 us

profile of v1, /device:TPU:1, one launch (start us, length us, event | category | flops | bytes accessed | tf_op | source)
XLA Modules:
  0.0 98.4 jit_solution(7960770761055915748)
XLA Ops:
  0.6 2.7 %shard_map.59 = (f32[32,32,128]{2,1,0:T(8,128)}, s32[128]{0:T(128)}, s32[128]{0:T(128)}) custom-call(s32[128]{0:T(128)} %bitcast.3, f32[3,128,128]{2,1,0:T(8,128)} %force_ref.1, s32[128,128]{1,0:T(8,128)} %cell_ref.1), custom_call_target="tpu_custom_call" | custom-call | tf_op jit(solution)/shard_map/pallas_call | solution.py:381
  3.3 0.0 copy-start.1
  3.3 1.0 %copy-done.1 = f32[32,32,128]{2,1,0:T(8,128)S(1)} copy-done((f32[32,32,128]{2,1,0:T(8,128)S(1)}, f32[32,32,128]{2,1,0:T(8,128)}, u32[]{:S(2)}) %copy-start.1) | copy-done | bytes 524312
  4.4 19.3 %shard_map.60.in_ref = f32[32,32,128]{2,1,0:T(8,128)S(1)} custom-call(f32[32,32,128]{2,1,0:T(8,128)S(1)} %copy-done.1), custom_call_target="tpu_custom_call" | custom-call | tf_op jit(solution)/shard_map/pallas_call | solution.py:112
  23.7 0.0 copy-start.2
  23.7 14.7 %shard_map.61.spread_ref = f32[4,128,128]{2,1,0:T(8,128)S(1)} custom-call(f32[32,32,128]{2,1,0:T(8,128)S(1)} %shard_map.60.in_ref), custom_call_target="tpu_custom_call" | custom-call | tf_op jit(solution)/shard_map/pallas_call | solution.py:393
  38.4 0.0 copy-done.2
  38.4 25.0 %shard_map.62 = f32[3,8,16,128]{3,2,1,0:T(8,128)S(1)} custom-call(f32[3,8,16,128]{3,2,1,0:T(8,128)S(1)} %copy-done.2, f32[4,128,128]{2,1,0:T(8,128)S(1)} %shard_map.61.spread_ref), custom_call_target="tpu_custom_call" | custom-call | tf_op jit(solution)/shard_map/pallas_call | solution.py:402
  63.5 13.0 %shard_map.63.src_ref = f32[32,24,128]{2,1,0:T(8,128)S(1)} custom-call(f32[32,32,128]{2,1,0:T(8,128)S(1)} %shard_map.60.in_ref, f32[3,128,128]{2,1,0:T(8,128)S(1)} %bitcast.2), custom_call_target="tpu_custom_call" | custom-call | tf_op jit(solution)/shard_map/pallas_call | solution.py:418
  76.5 18.5 %shard_map.64.in_ref = f32[32,24,128]{2,1,0:T(8,128)S(1)} custom-call(f32[32,24,128]{2,1,0:T(8,128)S(1)} %shard_map.63.src_ref), custom_call_target="tpu_custom_call" | custom-call | tf_op jit(solution)/shard_map/pallas_call | solution.py:112
  94.9 0.0 copy-start
  95.0 0.7 copy-done
  95.7 2.1 %shard_map.65 = f32[3,128,128]{2,1,0:T(8,128)} custom-call(s32[128]{0:T(128)} %get-tuple-element.6.dest_ref, s32[128]{0:T(128)} %get-tuple-element.7.rank_ref, f32[32,24,128]{2,1,0:T(8,128)} %copy-done), custom_call_target="tpu_custom_call" | custom-call | tf_op jit(solution)/shard_map/pallas_call | solution.py:426
  97.8 0.7 copy.7
Async XLA Ops:
  3.3 1.0 %copy-start.1 = (f32[32,32,128]{2,1,0:T(8,128)S(1)}, f32[32,32,128]{2,1,0:T(8,128)}, u32[]{:S(2)}) copy-start(f32[32,32,128]{2,1,0:T(8,128)} %get-tuple-element.5.src_ref) | copy-start | bytes 1572868
  23.7 14.7 %copy-start.2 = (f32[3,8,16,128]{3,2,1,0:T(8,128)S(1)}, f32[3,8,16,128]{3,2,1,0:T(8,128)}, u32[]{:S(2)}) copy-start(f32[3,8,16,128]{3,2,1,0:T(8,128)} %flow_ref.1) | copy-start | bytes 589828
  94.9 0.8 copy-start

commit v2 on v0

v2 whole, which is shorter than its diff:
```python
import functools

import jax
import jax.numpy as jnp
from jax import lax
from jax.experimental import pallas as pl
from jax.experimental.pallas import tpu as pltpu
from jax.sharding import PartitionSpec as P

SWEEPS = 4
STEPS = 2
MESH = pl.DeviceIdType.MESH

time_step = 0.5
viscosity = 0.2
stiffness = 1.0

HALO_X = SWEEPS + 2
HALO_Y = 8

BF = jnp.bfloat16
VMEM = pl.BlockSpec(memory_space=pltpu.VMEM)
SMEM = pl.BlockSpec(memory_space=pltpu.SMEM)
DIRECTIONS = [(i, j) for i in (-1, 0, 1) for j in (-1, 0, 1) if (i, j) != (0, 0)]


def pack_kernel(devices, cap, brick_ref, force_ref, cell_ref, out_ref, dest_ref, rank_ref, seen):
    blocks, width = cell_ref.shape
    out_ref[:, : 3 * cap, :] = jnp.zeros((devices, 3 * cap, width), jnp.float32)
    out_ref[:, 3 * cap :, :] = jnp.full((devices, cap, width), -1.0, jnp.float32)

    def clear(i, carry):
        seen[i] = 0
        return carry

    lax.fori_loop(0, devices, clear, 0)

    def place(b, carry):
        dest = brick_ref[b]
        rank = seen[dest]
        seen[dest] = rank + 1
        dest_ref[b] = dest
        rank_ref[b] = rank
        for c in range(3):
            out_ref[dest, pl.ds(c * cap + rank, 1), :] = force_ref[c, pl.ds(b, 1), :]
        out_ref[dest, pl.ds(3 * cap + rank, 1), :] = cell_ref[pl.ds(b, 1), :].astype(jnp.float32)
        return carry

    lax.fori_loop(0, blocks, place, 0, unroll=4)


def peer_of(me, k, devices, n_gy):
    peer = lax.rem(me + k, devices)
    return (peer // n_gy, lax.rem(peer, n_gy))


def cell_parts(cells, half, depth):
    row = cells // depth
    short = jnp.where(cells < 0, -1, lax.rem(row, half))
    long = (row // half) * depth + lax.rem(cells, depth)
    return short.astype(jnp.float32), long.astype(jnp.float32)


def tall(row):
    return jnp.broadcast_to(row, (16, row.shape[1])).astype(BF)


def one_hot_mask(row, size):
    shape = (size // 16, 16, row.shape[1])
    index = lax.broadcasted_iota(jnp.int32, shape, 0) * 16 + lax.broadcasted_iota(jnp.int32, shape, 1)
    return index.astype(jnp.float32).astype(BF) == tall(row)[None]


def spread_block(block, cap, half, depth):
    width = block.shape[1]
    short, long = cell_parts(block[3 * cap :].astype(jnp.int32), half, depth)
    high = block[: 3 * cap].astype(BF).astype(jnp.float32)
    low = block[: 3 * cap] - high
    zero = jnp.zeros((16, width), BF)[None]
    ones = jnp.ones((16, width), BF)[None]
    lefts, rights = [], []
    for e in range(cap):
        mask = one_hot_mask(short[e : e + 1], half)
        pieces = []
        for part in (high, low):
            for c in range(3):
                value = tall(part[c * cap + e : c * cap + e + 1])
                pieces.append(jnp.where(mask, value[None], zero).reshape(half, width))
        pieces.append(jnp.where(mask, ones, zero).reshape(half, width))
        lefts.append(jnp.concatenate(pieces, axis=0))
        spot = one_hot_mask(long[e : e + 1], 2 * depth)
        rights.append(jnp.where(spot, ones, zero).reshape(2 * depth, width))
    left = jnp.concatenate(lefts, axis=1)
    right = jnp.concatenate(rights, axis=1)
    return lax.dot_general(
        left, right, (((1,), (1,)), ((), ())), preferred_element_type=jnp.float32
    )


def pick_block(table, cell_rows, cap, half, depth):
    width = cell_rows.shape[1]
    index = lax.broadcasted_iota(jnp.int32, (half, width), 0).astype(jnp.float32)
    short, long = cell_parts(cell_rows.astype(jnp.int32), half, depth)
    zero = jnp.zeros((16, width), BF)[None]
    ones = jnp.ones((16, width), BF)[None]
    rights = []
    for e in range(cap):
        spot = one_hot_mask(long[e : e + 1], 2 * depth)
        rights.append(jnp.where(spot, ones, zero).reshape(2 * depth, width))
    both = jnp.dot(table, jnp.concatenate(rights, axis=1), preferred_element_type=jnp.float32)
    rows = []
    for c in range(3):
        for e in range(cap):
            cut = both[:, e * width : (e + 1) * width]
            value = cut[c * half : (c + 1) * half] + cut[(3 + c) * half : (4 + c) * half]
            mask = index == short[e : e + 1]
            rows.append(jnp.sum(jnp.where(mask, value, 0.0), axis=0, keepdims=True))
    return jnp.concatenate(rows, axis=0)


def flow_kernel(
    n_gx, n_gy, cap, dest_ref, rank_ref, sent_ref, flow_ref, out_ref, mark_ref,
    held, acc, spread, wide, wide_force, later, table, picked, back,
    halo_send, halo_recv, block_send, block_recv, back_send, back_recv, own_sem,
):
    size_x, size_y, depth = flow_ref.shape[1:]
    half = size_x * size_y // 2
    blocks = mark_ref.shape[1]
    devices = n_gx * n_gy
    gx, gy = lax.axis_index("gx"), lax.axis_index("gy")
    me = gx * n_gy + gy

    barrier = pltpu.get_barrier_semaphore()

    def greet(k, carry):
        pl.semaphore_signal(
            barrier, inc=1, device_id=peer_of(me, k, devices, n_gy), device_id_type=MESH
        )
        return carry

    lax.fori_loop(1, devices, greet, 0)
    own = pltpu.make_async_copy(sent_ref.at[me], held.at[me], own_sem)
    own.start()
    acc[...] = jnp.zeros_like(acc)
    pl.semaphore_wait(barrier, devices - 1)

    def remote(k, src, src_at, dst, dst_at, send_sem, recv_sem):
        return pltpu.make_async_remote_copy(
            src_ref=src.at[src_at],
            dst_ref=dst.at[dst_at],
            send_sem=send_sem.at[k],
            recv_sem=recv_sem.at[k],
            device_id=peer_of(me, k, devices, n_gy),
            device_id_type=MESH,
        )

    def block_to(k):
        return remote(k, sent_ref, lax.rem(me + k, devices), held, me, block_send, block_recv)

    def block_from(k):
        sender = lax.rem(me + devices - k, devices)
        return remote(k, sent_ref, sender, held, sender, block_send, block_recv)

    def back_to(k):
        return remote(k, picked, lax.rem(me + k, devices), back, me, back_send, back_recv)

    def back_from(k):
        sender = lax.rem(me + devices - k, devices)
        return remote(k, picked, sender, back, sender, back_send, back_recv)

    def exists(dx, dy):
        x, y = gx + dx, gy + dy
        return (x >= 0) & (x < n_gx) & (y >= 0) & (y < n_gy)

    def cut(d, size, halo, room):
        if d == 0:
            return (0, size), (room, size)
        if d > 0:
            return (size - halo, halo), (room - halo, halo)
        return (0, halo), (room + size, halo)

    def side(turn, number, src, target, halo):
        dx, dy = DIRECTIONS[number]
        (sx, nx), (tx, _) = cut(dx, size_x, halo, HALO_X)
        (sy, ny), (ty, _) = cut(dy, size_y, HALO_Y, HALO_Y)
        return pltpu.make_async_remote_copy(
            src_ref=src.at[:, pl.ds(sx, nx), pl.ds(sy, ny), :],
            dst_ref=target.at[:, pl.ds(tx, nx), pl.ds(ty, ny), :],
            send_sem=halo_send.at[turn, number],
            recv_sem=halo_recv.at[turn, number],
            device_id=(gx + dx, gy + dy),
            device_id_type=MESH,
        )

    inner = (slice(HALO_X, HALO_X + size_x), slice(HALO_Y, HALO_Y + size_y))

    def sides_begin(turn, src, target, halo):
        for number, (dx, dy) in enumerate(DIRECTIONS):

            @pl.when(exists(dx, dy))
            def _():
                side(turn, number, src, target, halo).start()

            @pl.when(jnp.logical_not(exists(-dx, -dy)))
            def _():
                _, (tx, nx) = cut(dx, size_x, halo, HALO_X)
                _, (ty, ny) = cut(dy, size_y, HALO_Y, HALO_Y)
                target[:, tx : tx + nx, ty : ty + ny, :] = jnp.zeros(
                    (target.shape[0], nx, ny, depth), jnp.float32
                )

        target[:, inner[0], inner[1], :] = src[...]

    def sides_arrive(turn, src, target, halo):
        for number, (dx, dy) in enumerate(DIRECTIONS):

            @pl.when(exists(-dx, -dy))
            def _():
                side(turn, number, src, target, halo).wait_recv()

    def sides_end(turn, src, target, halo):
        for number, (dx, dy) in enumerate(DIRECTIONS):

            @pl.when(exists(dx, dy))
            def _():
                side(turn, number, src, target, halo).wait_send()

    def begin(k, carry):
        block_to(k).start()
        return carry

    lax.fori_loop(1, devices, begin, 0)
    sides_begin(0, flow_ref, wide, HALO_X)

    own.wait()
    acc[...] += spread_block(held[me], cap, half, depth)

    def gather_in(k, carry):
        block_from(k).wait_recv()
        acc[...] += spread_block(held[lax.rem(me + devices - k, devices)], cap, half, depth)
        return carry

    lax.fori_loop(1, devices, gather_in, 0)
    for c in range(4):
        if c < 3:
            total = acc[c * half : (c + 1) * half] + acc[(3 + c) * half : (4 + c) * half]
        else:
            total = acc[6 * half : 7 * half]
        spread[c, : size_x // 2] = total[:, :depth].reshape(size_x // 2, size_y, depth)
        spread[c, size_x // 2 :] = total[:, depth:].reshape(size_x // 2, size_y, depth)

    wide_x, wide_y = size_x + 2 * HALO_X, size_y + 2 * HALO_Y
    place_x = lax.broadcasted_iota(jnp.int32, (wide_x, wide_y, depth), 0) + (gx * size_x - HALO_X)
    place_y = lax.broadcasted_iota(jnp.int32, (wide_x, wide_y, depth), 1) + (gy * size_y - HALO_Y)
    keep = (
        (place_x >= 0) & (place_x < n_gx * size_x) & (place_y >= 0) & (place_y < n_gy * size_y)
    ).astype(jnp.float32)
    level = lax.broadcasted_iota(jnp.int32, (1, wide_y, depth), 2)
    not_first = (level > 0).astype(jnp.float32)
    not_last = (level < depth - 1).astype(jnp.float32)

    def up_y(v):
        return pltpu.roll(v, wide_y - 1, 1)

    def down_y(v):
        return pltpu.roll(v, 1, 1)

    def up_z(v):
        return pltpu.roll(v, depth - 1, 2) * not_last

    def down_z(v):
        return pltpu.roll(v, 1, 2) * not_first

    def around(v):
        mid = v[1:-1]
        return (v[2:] + v[:-2]) + (up_y(mid) + down_y(mid)) + (up_z(mid) + down_z(mid))

    def advance(flow, force):
        provisional = []
        for c in range(3):
            mid = flow[c][1:-1]
            stepped = mid + time_step * (viscosity * (around(flow[c]) - 6.0 * mid) + force[c])
            provisional.append(stepped * keep[1:-1])
        p0, p1, p2 = provisional
        source = (0.5 / time_step) * (
            (p0[2:] - p0[:-2])
            + (up_y(p1[1:-1]) - down_y(p1[1:-1]))
            + (up_z(p2[1:-1]) - down_z(p2[1:-1]))
        )
        sixth = keep * (1.0 / 6.0)
        pressure = -source * sixth[2:-2]
        for sweep in range(1, SWEEPS):
            edge = sweep + 2
            pressure = (around(pressure) - source[sweep:-sweep]) * sixth[edge:-edge]
        mid = pressure[1:-1]
        slopes = (
            pressure[2:] - pressure[:-2],
            up_y(mid) - down_y(mid),
            up_z(mid) - down_z(mid),
        )
        far = HALO_X - 1
        return [
            (provisional[c][far:-far] - (0.5 * time_step) * slopes[c])[:, inner[1], :] for c in range(3)
        ]

    sides_begin(1, spread, wide_force, HALO_X - 1)
    sides_arrive(0, flow_ref, wide, HALO_X)
    sides_arrive(1, spread, wide_force, HALO_X - 1)
    result = advance([wide[c] for c in range(3)], [wide_force[c, 1:-1] for c in range(3)])
    for c in range(3):
        out_ref[c] = result[c]
    for turn in range(1, STEPS):
        sides_begin(turn + 1, out_ref, later, HALO_X)
        sides_arrive(turn + 1, out_ref, later, HALO_X)
        flow = [later[c] for c in range(3)]
        force = [wide_force[c, 1:-1] - stiffness * wide_force[3, 1:-1] * flow[c][1:-1] for c in range(3)]
        result = advance(flow, force)
        sides_end(turn + 1, out_ref, later, HALO_X)
        for c in range(3):
            out_ref[c] = result[c]

    for c in range(3):
        rows = result[c].reshape(2 * half, depth)
        flat = jnp.concatenate([rows[:half], rows[half:]], axis=1)
        high = flat.astype(BF)
        table[c * half : (c + 1) * half] = high
        table[(3 + c) * half : (4 + c) * half] = (flat - high.astype(jnp.float32)).astype(BF)

    def give_back(k, carry):
        peer = lax.rem(me + k, devices)
        picked[peer] = pick_block(table[...], held[peer, 3 * cap :, :], cap, half, depth)
        back_to(k).start()
        return carry

    lax.fori_loop(1, devices, give_back, 0)
    back[me] = pick_block(table[...], held[me, 3 * cap :, :], cap, half, depth)

    def finish(k, carry):
        block_to(k).wait_send()
        back_from(k).wait_recv()
        return carry

    lax.fori_loop(1, devices, finish, 0)

    def take(b, carry):
        dest = dest_ref[b]
        rank = rank_ref[b]
        for c in range(3):
            mark_ref[c, pl.ds(b, 1), :] = back[dest, pl.ds(c * cap + rank, 1), :]
        return carry

    lax.fori_loop(0, blocks, take, 0, unroll=4)

    def drain(k, carry):
        back_to(k).wait_send()
        return carry

    lax.fori_loop(1, devices, drain, 0)
    sides_end(0, flow_ref, wide, HALO_X)
    sides_end(1, spread, wide_force, HALO_X - 1)


def body(n_gx, n_gy, velocity, marker_force, marker_cell, block_brick):
    devices = n_gx * n_gy
    blocks, width = marker_cell.shape
    size_x, size_y, depth = velocity.shape[1:]
    cap = 2 * blocks // devices
    rows = size_x * size_y
    half = rows // 2
    sent, dest, rank = pl.pallas_call(
        functools.partial(pack_kernel, devices, cap),
        out_shape=(
            jax.ShapeDtypeStruct((devices, 4 * cap, width), jnp.float32),
            jax.ShapeDtypeStruct((blocks,), jnp.int32),
            jax.ShapeDtypeStruct((blocks,), jnp.int32),
        ),
        in_specs=[SMEM, VMEM, VMEM],
        out_specs=(VMEM, SMEM, SMEM),
        scratch_shapes=[pltpu.SMEM((devices,), jnp.int32)],
    )(block_brick.reshape(blocks), marker_force, marker_cell)
    wide = (size_x + 2 * HALO_X, size_y + 2 * HALO_Y, depth)
    many = pltpu.SemaphoreType.DMA((devices,))
    return pl.pallas_call(
        functools.partial(flow_kernel, n_gx, n_gy, cap),
        out_shape=(
            jax.ShapeDtypeStruct(velocity.shape, jnp.float32),
            jax.ShapeDtypeStruct((3, blocks, width), jnp.float32),
        ),
        in_specs=[SMEM, SMEM, VMEM, VMEM],
        out_specs=(VMEM, VMEM),
        scratch_shapes=[
            pltpu.VMEM(sent.shape, jnp.float32),
            pltpu.VMEM((7 * half, 2 * depth), jnp.float32),
            pltpu.VMEM((4, size_x, size_y, depth), jnp.float32),
            pltpu.VMEM((3,) + wide, jnp.float32),
            pltpu.VMEM((4,) + wide, jnp.float32),
            pltpu.VMEM((3,) + wide, jnp.float32),
            pltpu.VMEM((6 * half, 2 * depth), BF),
            pltpu.VMEM((devices, 3 * cap, width), jnp.float32),
            pltpu.VMEM((devices, 3 * cap, width), jnp.float32),
            pltpu.SemaphoreType.DMA((STEPS + 1, 8)),
            pltpu.SemaphoreType.DMA((STEPS + 1, 8)),
            many,
            many,
            many,
            many,
            pltpu.SemaphoreType.DMA,
        ],
        compiler_params=pltpu.CompilerParams(
            collective_id=0, has_side_effects=True, vmem_limit_bytes=40 << 20
        ),
    )(dest, rank, sent, velocity)


def solution(mesh):
    n_gx, n_gy = mesh.shape["gx"], mesh.shape["gy"]
    return jax.shard_map(
        functools.partial(body, n_gx, n_gy),
        mesh=mesh,
        in_specs=(
            P(None, "gx", "gy", None),
            P(None, ("gx", "gy"), None),
            P(("gx", "gy"), None),
            P(("gx", "gy"), None),
        ),
        out_specs=(P(None, "gx", "gy", None), P(None, ("gx", "gy"), None)),
        check_vma=False,
    )
```

time: 1720 us -> 68.1 us (0.04)
  other arithmetic: 1280 us -> 0 us
  starting transfers between devices: 235 us -> 0 us
  local copies, waits for them, and re-layouts: 168 us -> 3.05 us
  Pallas kernels: 0 us -> 64.1 us
  waiting for transfers between devices: 37 us -> 0 us
    scatter-add x2 -> x0, other arithmetic: 1260 us -> none  [body(): jnp.zeros((3, cell_total), jnp.float32).at[:, cell_flat]]
    ppermute x28 -> x0, starting transfers between devices: 207 us -> none  [the longest x14 183 us: with_halo(): lax.ppermute(lax.slice_in_dim(block, block.shape[dim] - width, None, axis...]
    gather x2 -> x0, local copies, waits for them, and re-layouts: 113 us -> none  [the longest x1 112 us: body(): picked = current.reshape(3, -1)[:, cell_flat].reshape(held_force.shape)]
    pallas_call x0 -> x2, Pallas kernels: none -> 64.1 us  [the longest x1 61.4 us: body(): pl.pallas_call(functools.partial(flow_kernel, n_gx, n_gy, cap), out_shape...]
    all_to_all x2 -> x0, starting transfers between devices: 27.4 us -> none  [the longest x1 20.3 us: send_back(): lax.all_to_all(shaped, ('gx', 'gy'), split_axis=1, concat_axis=1, tiled=T...]
    all_to_all x2 -> x0, waiting for transfers between devices: 22.3 us -> none  [the longest x1 12.7 us: send_back(): lax.all_to_all(shaped, ('gx', 'gy'), split_axis=1, concat_axis=1, tiled=T...]
  transfers between devices with their start and end apart: 30 -> 0, of which waited for: 16 -> 0; matrix products, arithmetic and copies ran while one was open for 14% -> 0% of each run, Pallas kernels for 0% -> 0%
where the time goes in v2:
time: 68.1 us; the launch traced here: 67.9 us
  Pallas kernels  64.1 us (94%)
  local copies, waits for them, and re-layouts  3.05 us (4%)
    pallas_call x1, Pallas kernels, body(): pl.pallas_call(functools.partial(flow_kernel, n_gx, n_gy, cap), out_shape...  61.4 us
    unnamed x10, local copies, waits for them, and re-layouts  3.05 us
    pallas_call x1, Pallas kernels, body(): pl.pallas_call(functools.partial(pack_kernel, devices, cap), out_shape=(j...  2.72 us

profile of v2, /device:TPU:1, one launch (start us, length us, event | category | flops | bytes accessed | tf_op | source)
XLA Modules:
  0.0 67.9 jit_solution(6651302727778594412)
XLA Ops:
  0.6 0.0 copy-start.1
  0.6 2.7 %shard_map.59 = (f32[32,32,128]{2,1,0:T(8,128)}, s32[128]{0:T(128)}, s32[128]{0:T(128)}) custom-call(s32[128]{0:T(128)} %bitcast.1, f32[3,128,128]{2,1,0:T(8,128)} %force_ref.1, s32[128,128]{1,0:T(8,128)} %cell_ref.1), custom_call_target="tpu_custom_call" | custom-call | tf_op jit(solution)/shard_map/pallas_call | solution.py:370
  3.4 0.0 copy-start.2
  3.4 0.0 copy-start.3
  3.4 0.0 copy-done.1
  3.4 0.6 copy-done.2
  4.0 0.0 copy-done.3
  4.0 0.0 copy-start
  4.0 1.0 %copy-done = f32[32,32,128]{2,1,0:T(8,128)S(1)} copy-done((f32[32,32,128]{2,1,0:T(8,128)S(1)}, f32[32,32,128]{2,1,0:T(8,128)}, u32[]{:S(2)}) %copy-start) | copy-done | bytes 524312
  5.1 61.4 %shard_map.60 = (f32[3,8,16,128]{3,2,1,0:T(8,128)S(1)}, f32[3,128,128]{2,1,0:T(8,128)S(1)}) custom-call(s32[128]{0:T(128)S(1)} %copy-done.2, s32[128]{0:T(128)S(1)} %copy-done.3, f32[32,32,128]{2,1,0:T(8,128)S(1)} %copy-done, f32[3,8,16,128]{3,2,1,0:T(8,128)S(1)} %copy-done.1), custom_call_target="tpu_custom_call" | custom-call | tf_op jit(solution)/shard_map/pallas_call | solution.py:383
  66.5 0.7 %copy.8 = f32[3,8,16,128]{3,2,1,0:T(8,128)} copy(f32[3,8,16,128]{3,2,1,0:T(8,128)S(1)} %get-tuple-element.10) | data formatting | bytes 393216
  67.2 0.7 copy.9
Async XLA Ops:
  0.6 2.8 %copy-start.1 = (f32[3,8,16,128]{3,2,1,0:T(8,128)S(1)}, f32[3,8,16,128]{3,2,1,0:T(8,128)}, u32[]{:S(2)}) copy-start(f32[3,8,16,128]{3,2,1,0:T(8,128)} %flow_ref.1) | copy-start | bytes 589828
  3.4 0.7 copy-start.2
  3.4 0.7 copy-start.3
  4.0 1.0 %copy-start = (f32[32,32,128]{2,1,0:T(8,128)S(1)}, f32[32,32,128]{2,1,0:T(8,128)}, u32[]{:S(2)}) copy-start(f32[32,32,128]{2,1,0:T(8,128)} %get-tuple-element.7.sent_ref) | copy-start | bytes 1572868

commit v3 on v2

--- a/solution.py
+++ b/solution.py
@@ -120,7 +120,7 @@
 
 def flow_kernel(
     n_gx, n_gy, cap, dest_ref, rank_ref, sent_ref, flow_ref, out_ref, mark_ref,
-    held, acc, spread, wide, wide_force, later, table, picked, back,
+    held, acc, spread, wide, wide_force, later, table, picked, back, corner_out, corner_in,
     halo_send, halo_recv, block_send, block_recv, back_send, back_recv, own_sem,
 ):
     size_x, size_y, depth = flow_ref.shape[1:]
@@ -179,8 +179,25 @@
             return (size - halo, halo), (room - halo, halo)
         return (0, halo), (room + size, halo)
 
+    def triangle(halo):
+        rows, first = [], 0
+        for i in range(1, halo):
+            rows.append((i, first, halo - i))
+            first += halo - i
+        return rows
+
     def side(turn, number, src, target, halo):
         dx, dy = DIRECTIONS[number]
+        if dx and dy:
+            fields = src.shape[0]
+            return pltpu.make_async_remote_copy(
+                src_ref=corner_out.at[turn, number, pl.ds(0, fields)],
+                dst_ref=corner_in.at[turn, number, pl.ds(0, fields)],
+                send_sem=halo_send.at[turn, number],
+                recv_sem=halo_recv.at[turn, number],
+                device_id=(gx + dx, gy + dy),
+                device_id_type=MESH,
+            )
         (sx, nx), (tx, _) = cut(dx, size_x, halo, HALO_X)
         (sy, ny), (ty, _) = cut(dy, size_y, HALO_Y, HALO_Y)
         return pltpu.make_async_remote_copy(
@@ -192,22 +209,54 @@
             device_id_type=MESH,
         )
 
+    def fill_corner(turn, number, src, halo):
+        dx, dy = DIRECTIONS[number]
+        fields = src.shape[0]
+        for i, first, n in triangle(halo):
+            x = size_x - i if dx > 0 else i - 1
+            y = size_y - n if dy > 0 else 0
+            corner_out[turn, number, :fields, first : first + n, :] = src[:, x, y : y + n, :]
+
+    def place_corner(turn, number, target, halo):
+        dx, dy = DIRECTIONS[number]
+        fields = target.shape[0]
+        for i, first, n in triangle(halo):
+            x = HALO_X - i if dx > 0 else HALO_X + size_x + i - 1
+            y = HALO_Y - n if dy > 0 else HALO_Y + size_y
+            target[:, x, y : y + n, :] = corner_in[turn, number, :fields, first : first + n, :]
+
     inner = (slice(HALO_X, HALO_X + size_x), slice(HALO_Y, HALO_Y + size_y))
 
     def sides_begin(turn, src, target, halo):
         for number, (dx, dy) in enumerate(DIRECTIONS):
-
-            @pl.when(exists(dx, dy))
-            def _():
-                side(turn, number, src, target, halo).start()
-
-            @pl.when(jnp.logical_not(exists(-dx, -dy)))
-            def _():
+            if not (dx and dy):
+
+                @pl.when(exists(dx, dy))
+                def _():
+                    side(turn, number, src, target, halo).start()
+
+        for number, (dx, dy) in enumerate(DIRECTIONS):
+            if dx and dy:
+                fill_corner(turn, number, src, halo)
+
+                @pl.when(exists(dx, dy))
+                def _():
+                    side(turn, number, src, target, halo).start()
+
                 _, (tx, nx) = cut(dx, size_x, halo, HALO_X)
                 _, (ty, ny) = cut(dy, size_y, HALO_Y, HALO_Y)
                 target[:, tx : tx + nx, ty : ty + ny, :] = jnp.zeros(
                     (target.shape[0], nx, ny, depth), jnp.float32
                 )
+            else:
+
+                @pl.when(jnp.logical_not(exists(-dx, -dy)))
+                def _():
+                    _, (tx, nx) = cut(dx, size_x, halo, HALO_X)
+                    _, (ty, ny) = cut(dy, size_y, HALO_Y, HALO_Y)
+                    target[:, tx : tx + nx, ty : ty + ny, :] = jnp.zeros(
+                        (target.shape[0], nx, ny, depth), jnp.float32
+                    )
 
         target[:, inner[0], inner[1], :] = src[...]
 
@@ -217,6 +266,8 @@
             @pl.when(exists(-dx, -dy))
             def _():
                 side(turn, number, src, target, halo).wait_recv()
+                if dx and dy:
+                    place_corner(turn, number, target, halo)
 
     def sides_end(turn, src, target, halo):
         for number, (dx, dy) in enumerate(DIRECTIONS):
@@ -398,6 +449,8 @@
             pltpu.VMEM((6 * half, 2 * depth), BF),
             pltpu.VMEM((devices, 3 * cap, width), jnp.float32),
             pltpu.VMEM((devices, 3 * cap, width), jnp.float32),
+            pltpu.VMEM((STEPS + 1, 8, 4, 16, depth), jnp.float32),
+            pltpu.VMEM((STEPS + 1, 8, 4, 16, depth), jnp.float32),
             pltpu.SemaphoreType.DMA((STEPS + 1, 8)),
             pltpu.SemaphoreType.DMA((STEPS + 1, 8)),
             many,

time: 68.1 us -> 64.5 us (0.947)
  Pallas kernels: 64.1 us -> 60.6 us
    pallas_call x1, Pallas kernels: 61.4 us -> 57.8 us  [body(): pl.pallas_call(functools.partial(flow_kernel, n_gx, n_gy, cap), out_shape...]
where the time goes in v3:
time: 64.5 us; the launch traced here: 64.3 us
  Pallas kernels  60.6 us (94%)
  local copies, waits for them, and re-layouts  3.05 us (5%)
  between operations  0.68 us (1%)
    pallas_call x1, Pallas kernels, body(): pl.pallas_call(functools.partial(flow_kernel, n_gx, n_gy, cap), out_shape...  57.8 us
    unnamed x10, local copies, waits for them, and re-layouts  3.05 us
    pallas_call x1, Pallas kernels, body(): pl.pallas_call(functools.partial(pack_kernel, devices, cap), out_shape=(j...  2.72 us

profile of v3, /device:TPU:1, one launch (start us, length us, event | category | flops | bytes accessed | tf_op | source)
XLA Modules:
  0.0 64.3 jit_solution(14510572277373779488)
XLA Ops:
  0.6 0.0 copy-start.1
  0.6 2.7 %shard_map.59 = (f32[32,32,128]{2,1,0:T(8,128)}, s32[128]{0:T(128)}, s32[128]{0:T(128)}) custom-call(s32[128]{0:T(128)} %bitcast.1, f32[3,128,128]{2,1,0:T(8,128)} %force_ref.1, s32[128,128]{1,0:T(8,128)} %cell_ref.1), custom_call_target="tpu_custom_call" | custom-call | tf_op jit(solution)/shard_map/pallas_call | solution.py:421
  3.4 0.0 copy-start.2
  3.4 0.0 copy-start.3
  3.4 0.0 copy-done.1
  3.4 0.6 copy-done.2
  4.0 0.0 copy-done.3
  4.0 0.0 copy-start
  4.0 1.0 %copy-done = f32[32,32,128]{2,1,0:T(8,128)S(1)} copy-done((f32[32,32,128]{2,1,0:T(8,128)S(1)}, f32[32,32,128]{2,1,0:T(8,128)}, u32[]{:S(2)}) %copy-start) | copy-done | bytes 524312
  5.1 57.8 %shard_map.60 = (f32[3,8,16,128]{3,2,1,0:T(8,128)S(1)}, f32[3,128,128]{2,1,0:T(8,128)S(1)}) custom-call(s32[128]{0:T(128)S(1)} %copy-done.2, s32[128]{0:T(128)S(1)} %copy-done.3, f32[32,32,128]{2,1,0:T(8,128)S(1)} %copy-done, f32[3,8,16,128]{3,2,1,0:T(8,128)S(1)} %copy-done.1), custom_call_target="tpu_custom_call" | custom-call | tf_op jit(solution)/shard_map/pallas_call | solution.py:434
  62.9 0.7 %copy.8 = f32[3,8,16,128]{3,2,1,0:T(8,128)} copy(f32[3,8,16,128]{3,2,1,0:T(8,128)S(1)} %get-tuple-element.10) | data formatting | bytes 393216
  63.6 0.7 %copy.9 = f32[3,128,128]{2,1,0:T(8,128)} copy(f32[3,128,128]{2,1,0:T(8,128)S(1)} %get-tuple-element.11) | data formatting | bytes 393216
Async XLA Ops:
  0.6 2.8 %copy-start.1 = (f32[3,8,16,128]{3,2,1,0:T(8,128)S(1)}, f32[3,8,16,128]{3,2,1,0:T(8,128)}, u32[]{:S(2)}) copy-start(f32[3,8,16,128]{3,2,1,0:T(8,128)} %flow_ref.1) | copy-start | bytes 589828
  3.4 0.7 %copy-start.2 = (s32[128]{0:T(128)S(1)}, s32[128]{0:T(128)}, u32[]{:S(2)}) copy-start(s32[128]{0:T(128)} %get-tuple-element.5.dest_ref) | copy-start | bytes 1540
  3.4 0.7 %copy-start.3 = (s32[128]{0:T(128)S(1)}, s32[128]{0:T(128)}, u32[]{:S(2)}) copy-start(s32[128]{0:T(128)} %get-tuple-element.6.rank_ref) | copy-start | bytes 1540
  4.0 1.0 %copy-start = (f32[32,32,128]{2,1,0:T(8,128)S(1)}, f32[32,32,128]{2,1,0:T(8,128)}, u32[]{:S(2)}) copy-start(f32[32,32,128]{2,1,0:T(8,128)} %get-tuple-element.7.sent_ref) | copy-start | bytes 1572868
